TPU v7x, 256 devices: a whole 4x4x8 slice. The times are simulated.
256 devices in a mesh: seq: 32 (over x, z), head: 8 (over y, core).
Axes of the slice: x: 4, y: 4, z: 8, core: 2. Of those that a mesh axis runs over, the one named last changes fastest.
Arguments:
- hidden: bfloat16 [32768, 8192], P('seq'), may hold values from -27 to 27, as said below
- key_value_weight: bfloat16 [8192, 2048], P('seq', 'head'), may hold values from -0.0625 to 0.0625
- down_projection: bfloat16 [2048, 512], P('head'), may hold values from -0.125 to 0.125
- up_projection: bfloat16 [512, 2048], P(None, 'head'), may hold values from -0.25 to 0.25
- positions: int32 [32768], P('seq'), may hold values from 0 to 131071
Outputs:
- grad_down: float32 [512, 2048], P('seq', 'head')
- grad_up: float32 [512, 2048], P('seq', 'head')
- rel_error: float32 [], replicated
Inputs may be any that keep to these rules, and one draw needn't show every extreme that they name: `hidden`: real-valued inputs, rows of differing scale.
All inputs are finite; a program needn't handle non-finite values.
Results may differ from a plain program's by a relative error of at most 0.0045.
Values may be sent and summed in bfloat16 or wider, within the bound.
No kernel may reach another device: no remote copies, remote signals or barrier semaphores. Data moves between devices by JAX's collectives and lax.ppermute only.
A program may use at most 64 MiB of HBM per device.

v0:
```python
import math

import jax
import jax.numpy as jnp
from jax import lax
from jax.sharding import PartitionSpec as P

KEY_VALUE_HEADS = 8
HEAD_SIZE = 128


THETA = 500000.0


def rotate_targets(dense, positions):
    half_dim = HEAD_SIZE // 2
    freqs = jnp.power(
        jnp.float32(THETA), -(jnp.arange(half_dim, dtype=jnp.float32) * 2.0 / HEAD_SIZE)
    )
    angle = positions.astype(jnp.float32)[:, None] * freqs[None, :]
    cosine = jnp.cos(angle)[:, None, :]
    sine = jnp.sin(angle)[:, None, :]
    shaped = dense.reshape(dense.shape[0], -1, 2, HEAD_SIZE)
    key_part = shaped[:, :, 0, :]
    first = key_part[..., :half_dim]
    second = key_part[..., half_dim:]
    turned = jnp.concatenate(
        [first * cosine - second * sine, second * cosine + first * sine], axis=-1
    )
    joined = jnp.stack([turned, shaped[:, :, 1, :]], axis=2)
    return joined.reshape(dense.shape[0], -1).astype(jnp.bfloat16)


def per_device(hidden, key_value_weight, down_projection, up_projection, positions):
    rows_here = hidden.shape[0]
    total_row_count = lax.axis_size("seq") * rows_here
    entry_items = total_row_count * 2 * KEY_VALUE_HEADS * HEAD_SIZE
    dense = jnp.dot(
        hidden,
        lax.all_gather(key_value_weight, "seq", axis=0, tiled=True),
        preferred_element_type=jnp.float32,
    )
    targets = rotate_targets(dense, positions)
    target_wide = targets.astype(jnp.float32)
    energy_local = jnp.sum(target_wide * target_wide)
    energy = lax.psum(energy_local, ("seq", "head"))
    factor = -(entry_items / energy) / math.sqrt(total_row_count)
    partial_value = jnp.dot(targets, down_projection, preferred_element_type=jnp.float32)
    latent = lax.psum(partial_value, "head").astype(jnp.bfloat16)
    rebuilt = jnp.dot(latent, up_projection, preferred_element_type=jnp.float32)
    residual = target_wide - rebuilt
    misfit_local = jnp.sum(residual * residual)
    latent_wide = latent.astype(jnp.float32)
    up_wide = up_projection.astype(jnp.float32)
    grad_up = lax.dot_general(
        latent_wide,
        residual,
        (((0,), (0,)), ((), ())),
        precision=lax.Precision.HIGHEST,
        preferred_element_type=jnp.float32,
    )
    local_grad = lax.dot_general(
        residual,
        up_wide,
        (((1,), (1,)), ((), ())),
        precision=lax.Precision.HIGHEST,
        preferred_element_type=jnp.float32,
    )
    d_latent = lax.psum(local_grad, "head").astype(jnp.bfloat16)
    grad_down = lax.dot_general(
        d_latent, targets, (((0,), (0,)), ((), ())), preferred_element_type=jnp.float32
    )
    grad_down = factor * grad_down
    grad_up = factor * grad_up
    grad_down, grad_up = (
        lax.psum_scatter(grad_down, "seq", scatter_dimension=0, tiled=True),
        lax.psum_scatter(grad_up, "seq", scatter_dimension=0, tiled=True),
    )
    misfit = lax.psum(misfit_local, ("seq", "head"))
    rel_error = misfit / energy
    return (grad_down, grad_up, rel_error)


def solution(mesh):
    return jax.shard_map(
        per_device,
        mesh=mesh,
        in_specs=(P("seq", None), P("seq", "head"), P("head", None), P(None, "head"), P("seq")),
        out_specs=(P("seq", "head"), P("seq", "head"), P()),
        check_vma=False,
    )
```

profile of v0, /device:TPU:32, one launch (start us, length us, event | category | flops | bytes accessed | tf_op | source)
XLA Modules:
  0.0 675.7 jit_solution(1749339733045724510)
XLA Ops:
  7.2 0.0 copy-start
  7.2 0.0 all-gather.2.cloned.1.call-start
  7.2 0.7 all-gather.2.cloned.1.call-update
  7.9 0.0 reduce-scatter.5.cloned.1.call-start
  8.0 0.7 convert_element_type.36
  8.7 86.5 %all-gather.2.cloned.1.call-done = bf16[8192,256]{1,0:T(8,128)(2,1)} async-done(((bf16[256,256]{1,0:T(8,128)(2,1)}), bf16[8192,256]{1,0:T(8,128)(2,1)}) %all-gather.2.cloned.1.call-update) | async-done | bytes 4194320 | tf_op jit(solution)/shard_map/all_gather | solution.py:40
  95.2 9.3 %fusion.9 = f32[1024,256]{0,1:T(8,128)S(1)} fusion(bf16[1024,8192]{1,0:T(8,128)(2,1)} %param.5, bf16[8192,256]{1,0:T(8,128)(2,1)} %all-gather.2.cloned.1.call-done), kind=kOutput, calls=%fused_computation.20 | convolution fusion | flops 4294967296 | bytes 22020096 | tf_op jit(solution)/shard_map/dot_general | solution.py:38
  104.6 0.0 copy-start.3
  104.6 1.2 fusion.7
  105.8 0.9 multiply_reduce_fusion.1
  106.7 1.0 copy.9
  107.7 0.5 fusion.10
  108.2 52.1 %all-reduce.3 = bf16[1024,512]{1,0:T(8,128)(2,1)S(1)} all-reduce(f32[1024,512]{1,0:T(8,128)S(1)} %fusion.10), channel_id=1, replica_groups=mesh['seq'=32,'head'=8] {'head'}, use_global_device_ids=true, to_apply=%region_2.0 | all-reduce | flops 524288 | bytes 3145728 | tf_op jit(solution)/shard_map/psum | solution.py:49
  160.3 2.1 multiply_reduce_fusion
  162.4 74.8 %all-reduce = (f32[]{:T(128)}, f32[]{:T(128)}) all-reduce(f32[]{:T(128)} %get-tuple-element.5, f32[]{:T(128)} %get-tuple-element.9), channel_id=1, replica_groups=mesh['seq'=32,'head'=8] {'seq','head'}, use_global_device_ids=true, to_apply=%region_1.0 | all-reduce | flops 2 | bytes 16 | tf_op jit(solution)/shard_map/psum | solution.py:46
  237.9 2.4 fusion.11
  240.3 2.1 convolution_multiply_fusion.1
  242.4 0.0 reduce-scatter.5.cloned.1.call-update
  242.4 0.0 reduce-scatter.3.cloned.1.call-start
  242.4 54.8 %all-reduce.4 = bf16[1024,512]{1,0:T(8,128)(2,1)S(1)} all-reduce(f32[1024,512]{1,0:T(8,128)} %fusion.11), channel_id=1, replica_groups=mesh['seq'=32,'head'=8] {'head'}, use_global_device_ids=true, to_apply=%region_3.0 | all-reduce | flops 524288 | bytes 3145728 | tf_op jit(solution)/shard_map/psum | solution.py:69
  297.3 1.3 convolution_multiply_fusion
  298.6 0.0 reduce-scatter.3.cloned.1.call-update
  299.8 152.0 %reduce-scatter.5.cloned.1.call-done = f32[16,256]{1,0:T(8,128)} async-done(((f32[512,256]{1,0:T(8,128)}), f32[16,256]{1,0:T(8,128)}) %reduce-scatter.5.cloned.1.call-update) | async-done | bytes 16400 | tf_op jit(solution)/shard_map/reduce_scatter | solution.py:77
  451.8 216.3 %reduce-scatter.3.cloned.1.call-done = f32[16,256]{1,0:T(8,128)} async-done(((f32[512,256]{1,0:T(8,128)}), f32[16,256]{1,0:T(8,128)}) %reduce-scatter.3.cloned.1.call-update) | async-done | bytes 16400 | tf_op jit(solution)/shard_map/reduce_scatter | solution.py:76
  (10 shorter events, 0.1 us)
Async XLA Ops:
  7.2 153.1 %copy-start = (bf16[512,256]{1,0:T(8,128)(2,1)S(1)}, bf16[512,256]{1,0:T(8,128)(2,1)}, u32[]{:S(2)}) copy-start(bf16[512,256]{1,0:T(8,128)(2,1)} %param.8) | copy-start | bytes 786436
  7.2 88.0 %all-gather.2.cloned.1.call-start = ((), (), s32[]{:S(2)}) async-start(), calls=%async_computation.2 | async-start | bytes 4325376 | tf_op jit(solution)/shard_map/all_gather | solution.py:40
  7.9 443.9 %reduce-scatter.5.cloned.1.call-start = ((), (), s32[]{:S(2)}) async-start(), calls=%async_computation.4 | async-start | bytes 540672 | tf_op jit(solution)/shard_map/reduce_scatter | solution.py:77
  104.6 3.2 copy-start.3
  106.7 1.0 copy-start.1
  237.9 59.4 %copy-start.2 = (bf16[1024,1,2,128]{0,3,2,1:T(8,128)(2,1)S(1)}, bf16[1024,1,2,128]{0,3,2,1:T(8,128)(2,1)}, u32[]{:S(2)}) copy-start(bf16[1024,1,2,128]{0,3,2,1:T(8,128)(2,1)} %copy-done.1) | copy-start | bytes 1572868
  242.4 425.7 %reduce-scatter.3.cloned.1.call-start = ((), (), s32[]{:S(2)}) async-start(), calls=%async_computation.3 | async-start | bytes 540672 | tf_op jit(solution)/shard_map/reduce_scatter | solution.py:76
Sparse Core Ops, SparseCore 0:
  10.6 84.5 all-gather.1
  242.5 209.2 reduce-scatter.4
  456.7 211.3 reduce-scatter.2
where the time goes:
time: 677 us; the launch traced here: 676 us
  waiting for transfers between devices  456 us (67%)
  blocking collectives  182 us (27%)
  matrix products  17.7 us (3%)
  between operations  16.9 us (2%)
    reduce_scatter x1, waiting for transfers between devices, per_device(): lax.psum_scatter(grad_down, 'seq', scatter_dimension=0, tiled=True)  216 us
    reduce_scatter x1, waiting for transfers between devices, per_device(): lax.psum_scatter(grad_up, 'seq', scatter_dimension=0, tiled=True)  152 us
    all_gather x1, waiting for transfers between devices, per_device(): lax.all_gather(key_value_weight, 'seq', axis=0, tiled=True)  86.5 us
    psum x1, blocking collectives, per_device(): energy = lax.psum(energy_local, ('seq', 'head'))  74.8 us
    psum x1, blocking collectives, per_device(): d_latent = lax.psum(local_grad, 'head').astype(jnp.bfloat16)  54.8 us
    psum x1, blocking collectives, per_device(): latent = lax.psum(partial_value, 'head').astype(jnp.bfloat16)  52.1 us
  transfers between devices with their start and end apart: 3, of which 3 were waited for; matrix products, arithmetic and copies ran while one was open for 0% of the time, Pallas kernels for 0%

commit v1 on v0

v1 whole, which is shorter than its diff:
```python
import math

import jax
import jax.numpy as jnp
from jax import lax
from jax.experimental import pallas as pl
from jax.experimental.pallas import tpu as pltpu
from jax.sharding import PartitionSpec as P

KEY_VALUE_HEADS = 8
HEAD_SIZE = 128
HEAD_COLUMNS = 2 * HEAD_SIZE
LATENT_RANK = 512
THETA = 500000.0
X, Z, HEADS = 4, 8, 8
SEQ = X * Z
MIB = 1024 * 1024
F32 = jnp.float32
BF16 = jnp.bfloat16


def z_shift(k):
    return [(x * Z + z, x * Z + (z + k) % Z) for x in range(X) for z in range(Z)]


def x_shift(k):
    return [(x * Z + z, ((x + k) % X) * Z + z) for x in range(X) for z in range(Z)]


def ring_z(own):
    up = down = own
    found = [(0, own)]
    for k in range(1, Z // 2):
        up, down = lax.ppermute(up, "seq", z_shift(1)), lax.ppermute(down, "seq", z_shift(-1))
        found += [(-k, up), (k, down)]
    half = own.shape[0] // 2
    first = lax.ppermute(up[:half], "seq", z_shift(1))
    second = lax.ppermute(down[half:], "seq", z_shift(-1))
    return found, (first, second)


def ring_x(own):
    up, down = lax.ppermute(own, "seq", x_shift(1)), lax.ppermute(own, "seq", x_shift(-1))
    half = own.shape[0] // 2
    first = lax.ppermute(up[:half], "seq", x_shift(1))
    second = lax.ppermute(down[half:], "seq", x_shift(-1))
    return [(0, own), (-1, up), (1, down)], (first, second)


def gather_weight(weight):
    part_rows = weight.shape[0] // 2
    part_a, part_b = weight[:part_rows], weight[part_rows:]
    a_found, a_far = ring_z(part_a)
    b_found, b_far = ring_x(part_b)
    a_order = [d for d, _ in a_found] + [Z // 2]
    b_order = [d for d, _ in b_found] + [X // 2]
    a_all = jnp.concatenate([rows for _, rows in a_found] + list(a_far), axis=0)
    b_all = jnp.concatenate([rows for _, rows in b_found] + list(b_far), axis=0)
    pieces = []
    found, (first, second) = ring_x(a_all)
    for dx, rows in found:
        pieces.append((rows, [(i * part_rows, dx, dz, 0) for i, dz in enumerate(a_order)]))
    half = len(a_order) // 2
    for rows, order in ((first, a_order[:half]), (second, a_order[half:])):
        pieces.append((rows, [(i * part_rows, X // 2, dz, 0) for i, dz in enumerate(order)]))
    found, (first, second) = ring_z(b_all)
    for dz, rows in found:
        pieces.append((rows, [(i * part_rows, dx, dz, 1) for i, dx in enumerate(b_order)]))
    half = len(b_order) // 2
    for rows, order in ((first, b_order[:half]), (second, b_order[half:])):
        pieces.append((rows, [(i * part_rows, dx, Z // 2, 1) for i, dx in enumerate(order)]))
    return pieces


def dense_targets(place, hidden, pieces, cosine, sine):
    rows, width = hidden.shape
    tile = 256
    count = len(pieces)

    def kernel(place_ref, hidden_ref, cos_ref, sin_ref, *rest):
        piece_refs, out_ref, weight_ref = rest[:count], rest[count], rest[count + 1]

        @pl.when(pl.program_id(0) == 0)
        def _():
            here = place_ref[0]
            x, z = here // Z, here % Z
            for ref, (_, entries) in zip(piece_refs, pieces):
                for row, dx, dz, part in entries:
                    owner = ((x + dx + X) % X) * Z + (z + dz + Z) % Z
                    start = pl.multiple_of(owner * 256 + part * 128, 128)
                    weight_ref[pl.ds(start, 128), :] = ref[row : row + 128, :]

        dense = jnp.dot(hidden_ref[...], weight_ref[...], preferred_element_type=F32)
        keys = dense[:, :HEAD_SIZE]
        turned = keys * cos_ref[...] + pltpu.roll(keys, HEAD_SIZE // 2, 1) * sin_ref[...]
        out_ref[:, :HEAD_SIZE] = turned.astype(BF16)
        out_ref[:, HEAD_SIZE:] = dense[:, HEAD_SIZE:].astype(BF16)

    whole = pl.BlockSpec(memory_space=pltpu.VMEM)
    return pl.pallas_call(
        kernel,
        grid=(rows // tile,),
        out_shape=jax.ShapeDtypeStruct((rows, HEAD_COLUMNS), BF16),
        in_specs=[
            pl.BlockSpec(memory_space=pltpu.SMEM),
            pl.BlockSpec((tile, width), lambda i: (i, 0)),
            pl.BlockSpec((tile, HEAD_SIZE), lambda i: (i, 0)),
            pl.BlockSpec((tile, HEAD_SIZE), lambda i: (i, 0)),
        ]
        + [whole] * count,
        out_specs=pl.BlockSpec((tile, HEAD_COLUMNS), lambda i: (i, 0)),
        scratch_shapes=[pltpu.VMEM((width, HEAD_COLUMNS), BF16)],
        compiler_params=pltpu.CompilerParams(vmem_limit_bytes=40 * MIB),
    )(place, hidden, cosine, sine, *[rows_ for rows_, _ in pieces])


def split3(value):
    high = value.astype(BF16).astype(F32)
    middle = (value - high).astype(BF16).astype(F32)
    return high, middle, value - high - middle


def spread(lane, first, second):
    out = jnp.zeros(lane.shape, F32)
    for i, part in enumerate((*split3(first), *split3(second))):
        out = jnp.where(lane == i, part, out)
    return out


def token_share(targets, down, up):
    heads, tokens, columns = targets.shape
    rank = down.shape[1]

    def kernel(t_ref, d_ref, u_ref, out_ref):
        total = jnp.zeros((tokens, rank), F32)
        for h in range(heads):
            total += jnp.dot(t_ref[h], d_ref[h * columns : (h + 1) * columns, :], preferred_element_type=F32)
        latent = total.astype(BF16)
        grad = jnp.zeros((tokens, rank), F32)
        energy = jnp.zeros((tokens, columns), F32)
        misfit = jnp.zeros((tokens, columns), F32)
        nt = (((1,), (1,)), ((), ()))
        for h in range(heads):
            wide = t_ref[h].astype(F32)
            rest = wide - jnp.dot(latent, u_ref[h], preferred_element_type=F32)
            energy += wide * wide
            misfit += rest * rest
            high = rest.astype(BF16)
            low = (rest - high.astype(F32)).astype(BF16)
            grad += lax.dot_general(high, u_ref[h], nt, preferred_element_type=F32)
            grad += lax.dot_general(low, u_ref[h], nt, preferred_element_type=F32)
        out_ref[0:tokens, 0:rank] = latent
        out_ref[0:tokens, rank : 2 * rank] = grad.astype(BF16)
        lane = lax.broadcasted_iota(jnp.int32, (16, 2 * rank), 1)
        sums = spread(lane, jnp.sum(energy), jnp.sum(misfit))
        out_ref[tokens : tokens + 16, :] = sums.astype(BF16)

    whole = pl.BlockSpec(memory_space=pltpu.VMEM)
    return pl.pallas_call(
        kernel,
        out_shape=jax.ShapeDtypeStruct((tokens + 16, 2 * rank), BF16),
        in_specs=[whole] * 3,
        out_specs=whole,
        compiler_params=pltpu.CompilerParams(vmem_limit_bytes=24 * MIB),
    )(targets, down, up)


def factor_grads(latents, targets, up):
    shares, padded, width = latents.shape
    tokens = padded - 16
    rank, columns = up.shape
    rows = rank // SEQ
    tn = (((0,), (0,)), ((), ()))

    def kernel(lat_ref, t_ref, u_ref, out_ref):
        grad_down = jnp.zeros((rank, columns), F32)
        grad_up = jnp.zeros((rank, columns), F32)
        sums = jnp.zeros((1, 128), F32)
        for j in range(shares):
            latent = lat_ref[j, 0:tokens, 0:rank]
            grad = lat_ref[j, 0:tokens, rank : 2 * rank]
            block = t_ref[j * tokens : (j + 1) * tokens, :]
            rest = block.astype(F32) - jnp.dot(latent, u_ref[...], preferred_element_type=F32)
            high = rest.astype(BF16)
            low = (rest - high.astype(F32)).astype(BF16)
            grad_up += lax.dot_general(latent, high, tn, preferred_element_type=F32)
            grad_up += lax.dot_general(latent, low, tn, preferred_element_type=F32)
            grad_down += lax.dot_general(grad, block, tn, preferred_element_type=F32)
            sums += lat_ref[j, tokens : tokens + 16, 0:128].astype(F32)[0:1, :]
        lane = lax.broadcasted_iota(jnp.int32, (1, 128), 1)
        energy = jnp.sum(jnp.where(lane < 3, sums, 0.0))
        misfit = jnp.sum(jnp.where((lane >= 3) & (lane < 6), sums, 0.0))
        lane = lax.broadcasted_iota(jnp.int32, (rows, 128), 1)
        tail = spread(lane, energy, misfit).astype(BF16)
        for s in range(SEQ):
            out_ref[s, :, 0:columns] = grad_down[s * rows : (s + 1) * rows, :].astype(BF16)
            out_ref[s, :, columns : 2 * columns] = grad_up[s * rows : (s + 1) * rows, :].astype(BF16)
            out_ref[s, :, 2 * columns :] = tail

    whole = pl.BlockSpec(memory_space=pltpu.VMEM)
    return pl.pallas_call(
        kernel,
        out_shape=jax.ShapeDtypeStruct((SEQ, rows, 2 * columns + 128), BF16),
        in_specs=[whole] * 3,
        out_specs=whole,
        compiler_params=pltpu.CompilerParams(vmem_limit_bytes=24 * MIB),
    )(latents, targets, up)


def finish(parts, columns, tokens_all):
    blocks, rows, width = parts.shape
    entries = tokens_all * 2 * KEY_VALUE_HEADS * HEAD_SIZE

    def kernel(p_ref, down_ref, up_ref, rel_ref):
        total = jnp.zeros((rows, width), F32)
        for s in range(blocks):
            total += p_ref[s].astype(F32)
        tail = total[0:1, 2 * columns :]
        lane = lax.broadcasted_iota(jnp.int32, tail.shape, 1)
        energy = jnp.sum(jnp.where(lane < 3, tail, 0.0), keepdims=True)
        misfit = jnp.sum(jnp.where((lane >= 3) & (lane < 6), tail, 0.0), keepdims=True)
        factor = -(entries / energy) / math.sqrt(tokens_all)
        down_ref[...] = total[:, :columns] * factor
        up_ref[...] = total[:, columns : 2 * columns] * factor
        rel_ref[...] = misfit / energy

    whole = pl.BlockSpec(memory_space=pltpu.VMEM)
    return pl.pallas_call(
        kernel,
        out_shape=[
            jax.ShapeDtypeStruct((rows, columns), F32),
            jax.ShapeDtypeStruct((rows, columns), F32),
            jax.ShapeDtypeStruct((1, 1), F32),
        ],
        in_specs=[whole],
        out_specs=[whole] * 3,
    )(parts)


def per_device(hidden, key_value_weight, down_projection, up_projection, positions):
    rows_here = hidden.shape[0]
    tokens_all = lax.axis_size("seq") * rows_here
    down = lax.all_gather(down_projection, "head", axis=0, tiled=True)
    up = lax.all_gather(up_projection, "head", axis=0)
    half_dim = HEAD_SIZE // 2
    freqs = jnp.power(F32(THETA), -(jnp.arange(half_dim, dtype=F32) * 2.0 / HEAD_SIZE))
    angle = positions.astype(F32)[:, None] * freqs[None, :]
    cosine, sine = jnp.cos(angle), jnp.sin(angle)
    cosine = jnp.concatenate([cosine, cosine], axis=1)
    sine = jnp.concatenate([-sine, sine], axis=1)
    place = lax.axis_index("seq").astype(jnp.int32)[None]
    targets = dense_targets(place, hidden, gather_weight(key_value_weight), cosine, sine)
    shares = targets.reshape(HEADS, rows_here // HEADS, HEAD_COLUMNS)
    shares = lax.all_to_all(shares, "head", 0, 0)
    latents = lax.all_gather(token_share(shares, down, up), "head", axis=0)
    parts = factor_grads(latents, targets, up_projection)
    parts = lax.all_to_all(parts, "seq", 0, 0)
    grad_down, grad_up, rel_error = finish(parts, HEAD_COLUMNS, tokens_all)
    return grad_down, grad_up, rel_error.reshape(())


def solution(mesh):
    return jax.shard_map(
        per_device,
        mesh=mesh,
        in_specs=(P("seq", None), P("seq", "head"), P("head", None), P(None, "head"), P("seq")),
        out_specs=(P("seq", "head"), P("seq", "head"), P()),
        check_vma=False,
    )
```

time: 677 us -> 170 us (0.25)
  waiting for transfers between devices: 456 us -> 41 us
  blocking collectives: 182 us -> 45.4 us
  starting transfers between devices: 0.12 us -> 38.1 us
  matrix products: 17.7 us -> 0 us
  Pallas kernels: 0 us -> 17 us
  local copies, waits for them, and re-layouts: 1.08 us -> 9.22 us
    reduce_scatter x2 -> x0, waiting for transfers between devices: 368 us -> none  [the longest x1 216 us: per_device(): lax.psum_scatter(grad_down, 'seq', scatter_dimension=0, tiled=True)]
    psum x3 -> x0, blocking collectives: 182 us -> none  [the longest x1 74.8 us: per_device(): energy = lax.psum(energy_local, ('seq', 'head'))]
    all_gather x1 -> x3, waiting for transfers between devices: 86.5 us -> 24.7 us  [the longest x1 24.7 us: per_device(): latents = lax.all_gather(token_share(shares, down, up), 'head', axis=0)]
    all_to_all x0 -> x2, blocking collectives: none -> 45.4 us  [the longest x1 30.7 us: per_device(): parts = lax.all_to_all(parts, 'seq', 0, 0)]
    ppermute x0 -> x24, starting transfers between devices: none -> 38 us  [the longest x6 13.2 us: ring_z(): lax.ppermute(up, 'seq', z_shift(1))]
    dot_general x6 -> x0, matrix products: 17.7 us -> none  [the longest x1 9.35 us: per_device(): jnp.dot(hidden, lax.all_gather(key_value_weight, 'seq', axis=0, tiled=Tru...]
    pallas_call x0 -> x4, Pallas kernels: none -> 17 us  [the longest x1 9.03 us: dense_targets(): pl.pallas_call(kernel, grid=(rows // tile,), out_shape=jax.ShapeDtypeStru...]
    ppermute x0 -> x24, waiting for transfers between devices: none -> 14.9 us  [the longest x6 8 us: ring_z(): lax.ppermute(up, 'seq', z_shift(1))]
  transfers between devices with their start and end apart: 3 -> 27, of which waited for: 3 -> 10; matrix products, arithmetic and copies ran while one was open for 0% -> 4% of each run, Pallas kernels for 0% -> 5%
where the time goes in v1:
time: 170 us
  blocking collectives  45.4 us (27%)
  waiting for transfers between devices  41 us (24%)
  starting transfers between devices  38.1 us (22%)
  Pallas kernels  17 us (10%)
  between operations  13.9 us (8%)
  local copies, waits for them, and re-layouts  9.22 us (5%)
  other arithmetic  5.08 us (3%)
    all_to_all x1, blocking collectives, per_device(): parts = lax.all_to_all(parts, 'seq', 0, 0)  30.7 us
    all_gather x1, waiting for transfers between devices, per_device(): latents = lax.all_gather(token_share(shares, down, up), 'head', axis=0)  24.7 us
    all_to_all x1, blocking collectives, per_device(): shares = lax.all_to_all(shares, 'head', 0, 0)  14.7 us
    ppermute x6, starting transfers between devices, ring_z(): lax.ppermute(up, 'seq', z_shift(1))  13.2 us
    pallas_call x1, Pallas kernels, dense_targets(): pl.pallas_call(kernel, grid=(rows // tile,), out_shape=jax.ShapeDtypeStru...  9.03 us
    ppermute x6, waiting for transfers between devices, ring_z(): lax.ppermute(up, 'seq', z_shift(1))  8 us
    unnamed x28, local copies, waits for them, and re-layouts  6.82 us
    ppermute x6, starting transfers between devices, ring_z(): lax.ppermute(down, 'seq', z_shift(-1))  6.56 us
  transfers between devices with their start and end apart: 27, of which 10 were waited for; matrix products, arithmetic and copies ran while one was open for 4% of the time, Pallas kernels for 5%

profile of v1, /device:TPU:32, one launch (start us, length us, event | category | flops | bytes accessed | tf_op | source)
XLA Modules:
  0.0 169.8 jit_solution(7289877688660791782)
XLA Ops:
  12.9 1.9 %collective-permute-start = (bf16[128,256]{1,0:T(8,128)(2,1)S(1)}, bf16[128,256]{1,0:T(8,128)(2,1)S(1)}, u32[]{:S(2)}, u32[]{:S(2)}) collective-permute-start(bf16[128,256]{1,0:T(8,128)(2,1)S(1)} %get-tuple-element.12), channel_id=1, source_target_pairs={{0,8},{8,16},{16,24},{24,32},{32,40},{40,48},{48,56},{56,0},{64,72... | collective-permute-start | bytes 196616 | tf_op jit(solution)/shard_map/ppermute | solution.py:34
  15.4 3.0 %collective-permute-start.15 = (bf16[64,256]{1,0:T(8,128)(2,1)S(1)}, bf16[64,256]{1,0:T(8,128)(2,1)S(1)}, u32[]{:S(2)}, u32[]{:S(2)}) collective-permute-start(bf16[64,256]{1,0:T(8,128)(2,1)S(1)} %slice.45), channel_id=1, source_target_pairs={{0,192},{8,200},{16,208},{24,216},{32,224},{40,232},{48,240},{56,2... | collective-permute-start | bytes 98312 | tf_op jit(solution)/shard_map/ppermute | solution.py:46
  18.4 1.9 %collective-permute-start.2 = (bf16[128,256]{1,0:T(8,128)(2,1)S(1)}, bf16[128,256]{1,0:T(8,128)(2,1)S(1)}, u32[]{:S(2)}, u32[]{:S(2)}) collective-permute-start(bf16[128,256]{1,0:T(8,128)(2,1)S(1)} %collective-permute-done), channel_id=1, source_target_pairs={{0,8},{8,16},{16,24},{24,32},{32,40},{40,48},{48,56},{56,0},{64,72... | collective-permute-start | bytes 196616 | tf_op jit(solution)/shard_map/ppermute | solution.py:34
  20.3 1.9 %collective-permute-start.3 = (bf16[128,256]{1,0:T(8,128)(2,1)S(1)}, bf16[128,256]{1,0:T(8,128)(2,1)S(1)}, u32[]{:S(2)}, u32[]{:S(2)}) collective-permute-start(bf16[128,256]{1,0:T(8,128)(2,1)S(1)} %collective-permute-done.1), channel_id=1, source_target_pairs={{0,56},{8,0},{16,8},{24,16},{32,24},{40,32},{48,40},{56,48},{64,12... | collective-permute-start | bytes 196616 | tf_op jit(solution)/shard_map/ppermute | solution.py:34
  23.4 2.2 %collective-permute-start.17 = (bf16[512,256]{1,0:T(8,128)(2,1)S(1)}, bf16[512,256]{1,0:T(8,128)(2,1)S(1)}, u32[]{:S(2)}, u32[]{:S(2)}) collective-permute-start(bf16[512,256]{1,0:T(8,128)(2,1)S(1)} %constant_dynamic-update-slice_fusion.9.rest_5_), channel_id=1, source_target_pairs={{0,56},{8,0},{16,8},{24,16},{32,24},{40,32},{48,40},{56,48},{64,12... | collective-permute-start | bytes 786440 | tf_op jit(solution)/shard_map/ppermute | solution.py:34
  26.6 2.3 %collective-permute-start.5 = (bf16[128,256]{1,0:T(8,128)(2,1)S(1)}, bf16[128,256]{1,0:T(8,128)(2,1)S(1)}, u32[]{:S(2)}, u32[]{:S(2)}) collective-permute-start(bf16[128,256]{1,0:T(8,128)(2,1)S(1)} %collective-permute-done.3), channel_id=1, source_target_pairs={{0,56},{8,0},{16,8},{24,16},{32,24},{40,32},{48,40},{56,48},{64,12... | collective-permute-start | bytes 196616 | tf_op jit(solution)/shard_map/ppermute | solution.py:34
  28.9 2.5 %collective-permute-done.4 = bf16[128,256]{1,0:T(8,128)(2,1)S(1)} collective-permute-done((bf16[128,256]{1,0:T(8,128)(2,1)S(1)}, bf16[128,256]{1,0:T(8,128)(2,1)S(1)}, u32[]{:S(2)}, u32[]{:S(2)}) %collective-permute-start.4) | collective-permute-done | bytes 65568 | tf_op jit(solution)/shard_map/ppermute | solution.py:34
  32.5 2.2 %collective-permute-start.7 = (bf16[64,256]{1,0:T(8,128)(2,1)S(1)}, bf16[64,256]{1,0:T(8,128)(2,1)S(1)}, u32[]{:S(2)}, u32[]{:S(2)}) collective-permute-start(bf16[64,256]{1,0:T(8,128)(2,1)S(1)} %slice.41), channel_id=1, source_target_pairs={{0,56},{8,0},{16,8},{24,16},{32,24},{40,32},{48,40},{56,48},{64,12... | collective-permute-start | bytes 98312 | tf_op jit(solution)/shard_map/ppermute | solution.py:38
  37.5 3.2 %collective-permute-start.9 = (bf16[1024,256]{1,0:T(8,128)(2,1)S(1)}, bf16[1024,256]{1,0:T(8,128)(2,1)S(1)}, u32[]{:S(2)}, u32[]{:S(2)}) collective-permute-start(bf16[1024,256]{1,0:T(8,128)(2,1)S(1)} %constant_dynamic-update-slice_fusion.rest_0_), channel_id=1, source_target_pairs={{0,192},{8,200},{16,208},{24,216},{32,224},{40,232},{48,240},{56,2... | collective-permute-start | bytes 1572872 | tf_op jit(solution)/shard_map/ppermute | solution.py:43
  40.8 3.2 %collective-permute-start.18 = (bf16[512,256]{1,0:T(8,128)(2,1)S(1)}, bf16[512,256]{1,0:T(8,128)(2,1)S(1)}, u32[]{:S(2)}, u32[]{:S(2)}) collective-permute-start(bf16[512,256]{1,0:T(8,128)(2,1)S(1)} %collective-permute-done.16.rest_6_), channel_id=1, source_target_pairs={{0,8},{8,16},{16,24},{24,32},{32,40},{40,48},{48,56},{56,0},{64,72... | collective-permute-start | bytes 786440 | tf_op jit(solution)/shard_map/ppermute | solution.py:34
  44.1 5.5 %collective-permute-done.18.rest_8_ = bf16[512,256]{1,0:T(8,128)(2,1)S(1)} collective-permute-done((bf16[512,256]{1,0:T(8,128)(2,1)S(1)}, bf16[512,256]{1,0:T(8,128)(2,1)S(1)}, u32[]{:S(2)}, u32[]{:S(2)}) %collective-permute-start.18) | collective-permute-done | bytes 262176 | tf_op jit(solution)/shard_map/ppermute | solution.py:34
  49.5 4.1 %collective-permute-start.20 = (bf16[512,256]{1,0:T(8,128)(2,1)S(1)}, bf16[512,256]{1,0:T(8,128)(2,1)S(1)}, u32[]{:S(2)}, u32[]{:S(2)}) collective-permute-start(bf16[512,256]{1,0:T(8,128)(2,1)S(1)} %collective-permute-done.18.rest_8_), channel_id=1, source_target_pairs={{0,8},{8,16},{16,24},{24,32},{32,40},{40,48},{48,56},{56,0},{64,72... | collective-permute-start | bytes 786440 | tf_op jit(solution)/shard_map/ppermute | solution.py:34
  55.6 3.2 %collective-permute-start.11 = (bf16[512,256]{1,0:T(8,128)(2,1)}, bf16[512,256]{1,0:T(8,128)(2,1)}, u32[]{:S(2)}, u32[]{:S(2)}) collective-permute-start(bf16[512,256]{1,0:T(8,128)(2,1)} %slice.43), channel_id=1, source_target_pairs={{0,192},{8,200},{16,208},{24,216},{32,224},{40,232},{48,240},{56,2... | collective-permute-start | bytes 786440 | tf_op jit(solution)/shard_map/ppermute | solution.py:46
  58.8 3.1 %fusion = (f32[1024,64]{1,0:T(8,128)}, f32[1024,64]{1,0:T(8,128)}, f32[1024,64]{1,0:T(8,128)}) fusion(f32[64]{0:T(128)S(1)} %negate_power_fusion, f32[1024]{0:T(1024)S(1)} %convert_element_type.3), kind=kLoop, calls=%fused_computation.4 | loop fusion | flops 131072 | bytes 790784 | tf_op jit(solution)/shard_map/neg | solution.py:250
  62.0 2.3 %collective-permute-start.22 = (bf16[256,256]{1,0:T(8,128)(2,1)S(1)}, bf16[256,256]{1,0:T(8,128)(2,1)S(1)}, u32[]{:S(2)}, u32[]{:S(2)}) collective-permute-start(bf16[256,256]{1,0:T(8,128)(2,1)S(1)} %slice.46), channel_id=1, source_target_pairs={{0,8},{8,16},{16,24},{24,32},{32,40},{40,48},{48,56},{56,0},{64,72... | collective-permute-start | bytes 393224 | tf_op jit(solution)/shard_map/ppermute | solution.py:37
  64.4 1.9 %pad_maximum_fusion = (f32[1024,128]{1,0:T(8,128)S(1)}, f32[1024,128]{1,0:T(8,128)S(1)}) fusion(f32[1024,64]{1,0:T(8,128)} %get-tuple-element.15, f32[1024,64]{1,0:T(8,128)} %get-tuple-element.14, f32[1024,64]{1,0:T(8,128)} %get-tuple-element.13), kind=kLoop, calls=%fused_computation.2 | loop fusion | flops 262144 | bytes 1835008 | tf_op jit(solution)/shard_map/concatenate | solution.py:249
  67.0 2.3 %collective-permute-done.23.rest_13_ = bf16[256,256]{1,0:T(8,128)(2,1)S(1)} collective-permute-done((bf16[256,256]{1,0:T(8,128)(2,1)S(1)}, bf16[256,256]{1,0:T(8,128)(2,1)S(1)}, u32[]{:S(2)}, u32[]{:S(2)}) %collective-permute-start.23) | collective-permute-done | bytes 131104 | tf_op jit(solution)/shard_map/ppermute | solution.py:38
  71.2 9.0 %shard_map.76.t_ref = bf16[1024,256]{1,0:T(8,128)(2,1)S(1)} custom-call(s32[1]{0:T(128)} %bitcast.place_ref, bf16[1024,8192]{1,0:T(8,128)(2,1)} %hidden_ref.1, f32[1024,128]{1,0:T(8,128)S(1)} %get-tuple-element.16.cos_ref, f32[1024,128]{1,0:T(8,128)S(1)} %get-tuple-element.17.sin_ref, bf16[1024,256]{1,0:T(8,128)(2,1)S(1)} %constant_dynamic-update-slice_fusion.rest_0_, ...), custom_call_target="tpu_custom_call" | custom-call | tf_op jit(solution)/shard_map/pallas_call | solution.py:100
  80.3 14.7 %all_to_all.10.t_ref = bf16[8,128,256]{2,1,0:T(8,128)(2,1)S(1)} all-to-all(bf16[8,128,256]{2,1,0:T(8,128)(2,1)S(1)} %bitcast.5), channel_id=1, replica_groups=mesh['seq'=32,'head'=8] {'head'}, dimensions={0} | all-to-all | bytes 1048576 | tf_op jit(solution)/shard_map/all_to_all | solution.py:254
  98.2 3.6 %shard_map.77 = bf16[144,1024]{1,0:T(8,128)(2,1)} custom-call(bf16[8,128,256]{2,1,0:T(8,128)(2,1)S(1)} %all_to_all.10.t_ref, bf16[2048,512]{1,0:T(8,128)(2,1)S(1)} %copy-done.1, bf16[8,512,256]{2,1,0:T(8,128)(2,1)S(1)} %bitcast.7), custom_call_target="tpu_custom_call" | custom-call | tf_op jit(solution)/shard_map/pallas_call | solution.py:159
  101.8 24.7 %all-gather.10.cloned.1.call-done = bf16[1152,1024]{1,0:T(8,128)(2,1)} async-done(((bf16[144,1024]{1,0:T(8,128)(2,1)}), bf16[1152,1024]{1,0:T(8,128)(2,1)}) %all-gather.10.cloned.1.call-update) | async-done | bytes 2359312 | tf_op jit(solution)/shard_map/all_gather | solution.py:255
  128.2 2.5 %shard_map.78 = bf16[32,16,640]{2,1,0:T(8,128)(2,1)S(1)} custom-call(bf16[8,144,1024]{2,1,0:T(8,128)(2,1)S(1)} %bitcast.6, bf16[1024,256]{1,0:T(8,128)(2,1)S(1)} %shard_map.76.t_ref, bf16[512,256]{1,0:T(8,128)(2,1)S(1)} %copy-done.3), custom_call_target="tpu_custom_call" | custom-call | tf_op jit(solution)/shard_map/pallas_call | solution.py:201
  130.7 30.7 %all_to_all.11.p_ref = bf16[32,16,640]{2,1,0:T(8,128)(2,1)} all-to-all(bf16[32,16,640]{2,1,0:T(8,128)(2,1)S(1)} %shard_map.78), channel_id=1, replica_groups=mesh['seq'=32,'head'=8] {'seq'}, dimensions={0} | all-to-all | bytes 1310720 | tf_op jit(solution)/shard_map/all_to_all | solution.py:257
  161.4 1.9 %shard_map.79 = (f32[16,256]{1,0:T(8,128)}, f32[16,256]{1,0:T(8,128)}, f32[1,1]{1,0:T(1,128)}) custom-call(bf16[32,16,640]{2,1,0:T(8,128)(2,1)} %all_to_all.11.p_ref), custom_call_target="tpu_custom_call" | custom-call | tf_op jit(solution)/shard_map/pallas_call | solution.py:228
  (82 shorter events, 21.8 us)
Async XLA Ops:
  7.2 87.8 %all-gather.6.cloned.1.call-start = ((), (), s32[]{:S(2)}) async-start(), calls=%async_computation.2 | async-start | bytes 2359296 | tf_op jit(solution)/shard_map/all_gather | solution.py:243
  7.9 87.1 %all-gather.8.cloned.1.call-start = ((), (), s32[]{:S(2)}) async-start(), calls=%async_computation.3 | async-start | bytes 2359296 | tf_op jit(solution)/shard_map/all_gather | solution.py:244
  8.7 117.8 %all-gather.10.cloned.1.call-start = ((), (), s32[]{:S(2)}) async-start(), calls=%async_computation.4 | async-start | bytes 2654208 | tf_op jit(solution)/shard_map/all_gather | solution.py:255
  9.6 5.6 %collective-permute-start.12 = (bf16[128,256]{1,0:T(8,128)(2,1)S(1)}, bf16[128,256]{1,0:T(8,128)(2,1)S(1)}, u32[]{:S(2)}, u32[]{:S(2)}) collective-permute-start(bf16[128,256]{1,0:T(8,128)(2,1)S(1)} %get-tuple-element.9), channel_id=1, source_target_pairs={{0,64},{8,72},{16,80},{24,88},{32,96},{40,104},{48,112},{56,120},{... | collective-permute-start | bytes 196616 | tf_op jit(solution)/shard_map/ppermute | solution.py:43
  12.9 5.5 %collective-permute-start = (bf16[128,256]{1,0:T(8,128)(2,1)S(1)}, bf16[128,256]{1,0:T(8,128)(2,1)S(1)}, u32[]{:S(2)}, u32[]{:S(2)}) collective-permute-start(bf16[128,256]{1,0:T(8,128)(2,1)S(1)} %get-tuple-element.12), channel_id=1, source_target_pairs={{0,8},{8,16},{16,24},{24,32},{32,40},{40,48},{48,56},{56,0},{64,72... | collective-permute-start | bytes 196616 | tf_op jit(solution)/shard_map/ppermute | solution.py:34
  14.8 5.5 %collective-permute-start.1 = (bf16[128,256]{1,0:T(8,128)(2,1)S(1)}, bf16[128,256]{1,0:T(8,128)(2,1)S(1)}, u32[]{:S(2)}, u32[]{:S(2)}) collective-permute-start(bf16[128,256]{1,0:T(8,128)(2,1)S(1)} %get-tuple-element.12), channel_id=1, source_target_pairs={{0,56},{8,0},{16,8},{24,16},{32,24},{40,32},{48,40},{56,48},{64,12... | collective-permute-start | bytes 196616 | tf_op jit(solution)/shard_map/ppermute | solution.py:34
  15.2 7.1 %collective-permute-start.14 = (bf16[64,256]{1,0:T(8,128)(2,1)S(1)}, bf16[64,256]{1,0:T(8,128)(2,1)S(1)}, u32[]{:S(2)}, u32[]{:S(2)}) collective-permute-start(bf16[64,256]{1,0:T(8,128)(2,1)S(1)} %slice.44), channel_id=1, source_target_pairs={{0,64},{8,72},{16,80},{24,88},{32,96},{40,104},{48,112},{56,120},{... | collective-permute-start | bytes 98312 | tf_op jit(solution)/shard_map/ppermute | solution.py:45
  15.4 6.8 %collective-permute-start.15 = (bf16[64,256]{1,0:T(8,128)(2,1)S(1)}, bf16[64,256]{1,0:T(8,128)(2,1)S(1)}, u32[]{:S(2)}, u32[]{:S(2)}) collective-permute-start(bf16[64,256]{1,0:T(8,128)(2,1)S(1)} %slice.45), channel_id=1, source_target_pairs={{0,192},{8,200},{16,208},{24,216},{32,224},{40,232},{48,240},{56,2... | collective-permute-start | bytes 98312 | tf_op jit(solution)/shard_map/ppermute | solution.py:46
  18.4 7.2 %collective-permute-start.2 = (bf16[128,256]{1,0:T(8,128)(2,1)S(1)}, bf16[128,256]{1,0:T(8,128)(2,1)S(1)}, u32[]{:S(2)}, u32[]{:S(2)}) collective-permute-start(bf16[128,256]{1,0:T(8,128)(2,1)S(1)} %collective-permute-done), channel_id=1, source_target_pairs={{0,8},{8,16},{16,24},{24,32},{32,40},{40,48},{48,56},{56,0},{64,72... | collective-permute-start | bytes 196616 | tf_op jit(solution)/shard_map/ppermute | solution.py:34
  20.3 6.2 %collective-permute-start.3 = (bf16[128,256]{1,0:T(8,128)(2,1)S(1)}, bf16[128,256]{1,0:T(8,128)(2,1)S(1)}, u32[]{:S(2)}, u32[]{:S(2)}) collective-permute-start(bf16[128,256]{1,0:T(8,128)(2,1)S(1)} %collective-permute-done.1), channel_id=1, source_target_pairs={{0,56},{8,0},{16,8},{24,16},{32,24},{40,32},{48,40},{56,48},{64,12... | collective-permute-start | bytes 196616 | tf_op jit(solution)/shard_map/ppermute | solution.py:34
  22.3 18.5 %collective-permute-start.16 = (bf16[512,256]{1,0:T(8,128)(2,1)S(1)}, bf16[512,256]{1,0:T(8,128)(2,1)S(1)}, u32[]{:S(2)}, u32[]{:S(2)}) collective-permute-start(bf16[512,256]{1,0:T(8,128)(2,1)S(1)} %constant_dynamic-update-slice_fusion.9.rest_5_), channel_id=1, source_target_pairs={{0,8},{8,16},{16,24},{24,32},{32,40},{40,48},{48,56},{56,0},{64,72... | collective-permute-start | bytes 786440 | tf_op jit(solution)/shard_map/ppermute | solution.py:34
  23.4 20.6 %collective-permute-start.17 = (bf16[512,256]{1,0:T(8,128)(2,1)S(1)}, bf16[512,256]{1,0:T(8,128)(2,1)S(1)}, u32[]{:S(2)}, u32[]{:S(2)}) collective-permute-start(bf16[512,256]{1,0:T(8,128)(2,1)S(1)} %constant_dynamic-update-slice_fusion.9.rest_5_), channel_id=1, source_target_pairs={{0,56},{8,0},{16,8},{24,16},{32,24},{40,32},{48,40},{56,48},{64,12... | collective-permute-start | bytes 786440 | tf_op jit(solution)/shard_map/ppermute | solution.py:34
  25.6 5.8 %collective-permute-start.4 = (bf16[128,256]{1,0:T(8,128)(2,1)S(1)}, bf16[128,256]{1,0:T(8,128)(2,1)S(1)}, u32[]{:S(2)}, u32[]{:S(2)}) collective-permute-start(bf16[128,256]{1,0:T(8,128)(2,1)S(1)} %collective-permute-done.2), channel_id=1, source_target_pairs={{0,8},{8,16},{16,24},{24,32},{32,40},{40,48},{48,56},{56,0},{64,72... | collective-permute-start | bytes 196616 | tf_op jit(solution)/shard_map/ppermute | solution.py:34
  26.6 5.9 %collective-permute-start.5 = (bf16[128,256]{1,0:T(8,128)(2,1)S(1)}, bf16[128,256]{1,0:T(8,128)(2,1)S(1)}, u32[]{:S(2)}, u32[]{:S(2)}) collective-permute-start(bf16[128,256]{1,0:T(8,128)(2,1)S(1)} %collective-permute-done.3), channel_id=1, source_target_pairs={{0,56},{8,0},{16,8},{24,16},{32,24},{40,32},{48,40},{56,48},{64,12... | collective-permute-start | bytes 196616 | tf_op jit(solution)/shard_map/ppermute | solution.py:34
  31.4 5.1 %collective-permute-start.6 = (bf16[64,256]{1,0:T(8,128)(2,1)S(1)}, bf16[64,256]{1,0:T(8,128)(2,1)S(1)}, u32[]{:S(2)}, u32[]{:S(2)}) collective-permute-start(bf16[64,256]{1,0:T(8,128)(2,1)S(1)} %slice.40), channel_id=1, source_target_pairs={{0,8},{8,16},{16,24},{24,32},{32,40},{40,48},{48,56},{56,0},{64,72... | collective-permute-start | bytes 98312 | tf_op jit(solution)/shard_map/ppermute | solution.py:37
  32.5 5.0 %collective-permute-start.7 = (bf16[64,256]{1,0:T(8,128)(2,1)S(1)}, bf16[64,256]{1,0:T(8,128)(2,1)S(1)}, u32[]{:S(2)}, u32[]{:S(2)}) collective-permute-start(bf16[64,256]{1,0:T(8,128)(2,1)S(1)} %slice.41), channel_id=1, source_target_pairs={{0,56},{8,0},{16,8},{24,16},{32,24},{40,32},{48,40},{56,48},{64,12... | collective-permute-start | bytes 98312 | tf_op jit(solution)/shard_map/ppermute | solution.py:38
  37.5 16.6 %collective-permute-start.8 = (bf16[1024,256]{1,0:T(8,128)(2,1)S(1)}, bf16[1024,256]{1,0:T(8,128)(2,1)S(1)}, u32[]{:S(2)}, u32[]{:S(2)}) collective-permute-start(bf16[1024,256]{1,0:T(8,128)(2,1)S(1)} %constant_dynamic-update-slice_fusion.rest_0_), channel_id=1, source_target_pairs={{0,64},{8,72},{16,80},{24,88},{32,96},{40,104},{48,112},{56,120},{... | collective-permute-start | bytes 1572872 | tf_op jit(solution)/shard_map/ppermute | solution.py:43
  37.5 17.3 %collective-permute-start.9 = (bf16[1024,256]{1,0:T(8,128)(2,1)S(1)}, bf16[1024,256]{1,0:T(8,128)(2,1)S(1)}, u32[]{:S(2)}, u32[]{:S(2)}) collective-permute-start(bf16[1024,256]{1,0:T(8,128)(2,1)S(1)} %constant_dynamic-update-slice_fusion.rest_0_), channel_id=1, source_target_pairs={{0,192},{8,200},{16,208},{24,216},{32,224},{40,232},{48,240},{56,2... | collective-permute-start | bytes 1572872 | tf_op jit(solution)/shard_map/ppermute | solution.py:43
  40.8 8.8 %collective-permute-start.18 = (bf16[512,256]{1,0:T(8,128)(2,1)S(1)}, bf16[512,256]{1,0:T(8,128)(2,1)S(1)}, u32[]{:S(2)}, u32[]{:S(2)}) collective-permute-start(bf16[512,256]{1,0:T(8,128)(2,1)S(1)} %collective-permute-done.16.rest_6_), channel_id=1, source_target_pairs={{0,8},{8,16},{16,24},{24,32},{32,40},{40,48},{48,56},{56,0},{64,72... | collective-permute-start | bytes 786440 | tf_op jit(solution)/shard_map/ppermute | solution.py:34
  44.0 10.1 %collective-permute-start.19 = (bf16[512,256]{1,0:T(8,128)(2,1)S(1)}, bf16[512,256]{1,0:T(8,128)(2,1)S(1)}, u32[]{:S(2)}, u32[]{:S(2)}) collective-permute-start(bf16[512,256]{1,0:T(8,128)(2,1)S(1)} %collective-permute-done.17.rest_7_), channel_id=1, source_target_pairs={{0,56},{8,0},{16,8},{24,16},{32,24},{40,32},{48,40},{56,48},{64,12... | collective-permute-start | bytes 786440 | tf_op jit(solution)/shard_map/ppermute | solution.py:34
  49.5 12.4 %collective-permute-start.20 = (bf16[512,256]{1,0:T(8,128)(2,1)S(1)}, bf16[512,256]{1,0:T(8,128)(2,1)S(1)}, u32[]{:S(2)}, u32[]{:S(2)}) collective-permute-start(bf16[512,256]{1,0:T(8,128)(2,1)S(1)} %collective-permute-done.18.rest_8_), channel_id=1, source_target_pairs={{0,8},{8,16},{16,24},{24,32},{32,40},{40,48},{48,56},{56,0},{64,72... | collective-permute-start | bytes 786440 | tf_op jit(solution)/shard_map/ppermute | solution.py:34
  54.1 10.2 %collective-permute-start.21 = (bf16[512,256]{1,0:T(8,128)(2,1)S(1)}, bf16[512,256]{1,0:T(8,128)(2,1)S(1)}, u32[]{:S(2)}, u32[]{:S(2)}) collective-permute-start(bf16[512,256]{1,0:T(8,128)(2,1)S(1)} %collective-permute-done.19.rest_9_), channel_id=1, source_target_pairs={{0,56},{8,0},{16,8},{24,16},{32,24},{40,32},{48,40},{56,48},{64,12... | collective-permute-start | bytes 786440 | tf_op jit(solution)/shard_map/ppermute | solution.py:34
  54.9 11.5 %collective-permute-start.10 = (bf16[512,256]{1,0:T(8,128)(2,1)}, bf16[512,256]{1,0:T(8,128)(2,1)}, u32[]{:S(2)}, u32[]{:S(2)}) collective-permute-start(bf16[512,256]{1,0:T(8,128)(2,1)} %slice.42), channel_id=1, source_target_pairs={{0,64},{8,72},{16,80},{24,88},{32,96},{40,104},{48,112},{56,120},{... | collective-permute-start | bytes 786440 | tf_op jit(solution)/shard_map/ppermute | solution.py:45
  55.6 10.8 %collective-permute-start.11 = (bf16[512,256]{1,0:T(8,128)(2,1)}, bf16[512,256]{1,0:T(8,128)(2,1)}, u32[]{:S(2)}, u32[]{:S(2)}) collective-permute-start(bf16[512,256]{1,0:T(8,128)(2,1)} %slice.43), channel_id=1, source_target_pairs={{0,192},{8,200},{16,208},{24,216},{32,224},{40,232},{48,240},{56,2... | collective-permute-start | bytes 786440 | tf_op jit(solution)/shard_map/ppermute | solution.py:46
  (12 other events, 115.3 us)
Sparse Core Ops, SparseCore 0:
  9.9 30.3 all-gather.5
  42.1 28.0 all-gather.7
  101.9 24.5 all-gather.9
